TPU v7x, 32 devices: a whole 2x2x4 slice. The times are simulated.
32 devices in a mesh: groups: 2 (over x), gx: 16 (over z, y, core).
Axes of the slice: x: 2, y: 2, z: 4, core: 2. Of those that a mesh axis runs over, the one named last changes fastest.
Arguments:
- terminal: float32 [32, 128, 2048], P('groups', 'gx'), parts along dimension 0, may hold values from -6 to 6
- misfit: float32 [4, 32, 128, 2048], P(None, 'groups', 'gx'), parts along dimension 1, may hold values from -6 to 6
- material: int32 [16, 128, 16], P(None, 'gx'), may hold values from 0 to 7
- material_table: float32 [2, 8], replicated, may hold values from 0.3 to 1
- heater_slot: int32 [8192], replicated, may hold values from 0 to 8191, as said below
- entry_heater: int32 [32768], P('gx'), may hold values from 0 to 8191, as said below
- entry_block: int32 [32768], P('gx'), may hold values from 0 to 2047
- profile: float32 [32768, 128], P('gx'), may hold values from -0.5 to 0.5
Outputs:
- adjoint: float32 [32, 128, 2048], P('groups', 'gx'), parts along dimension 0
- heater_grad: float32 [16384], P(('groups', 'gx')), parts along dimension 0
There are 2 independent parts, one for each index of `groups`. A program takes and returns all parts, laid end to end along the dimension named above; an argument that names none is the same for every part. Nothing has to cross between parts.
Inputs may be any that keep to these rules, and one draw needn't show every extreme that they name: heater_slot is a permutation of the slots. `entry_heater`: among one device's 2048 entries, at most 256 have heaters whose slots lie on any one owning device, and on each device exactly 256 go to some owner.
All inputs are finite; a program needn't handle non-finite values.
Results may differ from a plain program's by a relative error of at most 0.00002.
Values sent between devices are 32-bit elements; how exact they have to be, the bound alone decides.
A program may use at most 64 MiB of HBM per device.

v0:
```python
import jax
import jax.numpy as jnp
from jax import lax
from jax.sharding import PartitionSpec as P


def extended_2(value, sides, width):
    for axis, dim in sides:
        peers, length = (lax.axis_size(axis), value.shape[dim])
        up = [(i, (i + 1) % peers) for i in range(peers - 1)]
        down = [(j, i) for i, j in up]
        last = lax.slice_in_dim(value, length - width, length, axis=dim)
        leading = lax.slice_in_dim(value, 0, width, axis=dim)
        before = lax.ppermute(last, axis, up)
        after = lax.ppermute(leading, axis, down)
        value = jnp.concatenate([before, value, after], axis=dim)
    return value


def operate(field, lateral, vertical, inside_x):
    center = field[:, 1:-1]
    own_lat = lateral[:, 1:-1]
    own_vert = vertical[:, 1:-1]
    summed = jnp.zeros_like(center)
    for lower, upper in ((2, None), (0, -2)):
        conductance = 0.5 * (own_lat + lateral[:, lower:upper]) * inside_x[:, lower:upper]
        summed = summed + conductance * (field[:, lower:upper] - center)
    edges = ((0, 0), (0, 0), (1, 1))
    field_y = jnp.pad(center, edges)
    lat_y = jnp.pad(own_lat, edges)
    open_y = jnp.pad(jnp.ones((1, 1, center.shape[2]), jnp.float32), edges)
    for lower, upper in ((2, None), (0, -2)):
        conductance = 0.5 * (own_lat + lat_y[:, :, lower:upper]) * open_y[:, :, lower:upper]
        summed = summed + conductance * (field_y[:, :, lower:upper] - center)
    edges_z = ((1, 1), (0, 0), (0, 0))
    field_z = jnp.pad(center, edges_z)
    vert_z = jnp.pad(own_vert, edges_z)
    open_z = jnp.pad(jnp.ones((center.shape[0], 1, 1), jnp.float32), edges_z)
    for lower, upper in ((2, None), (0, -2)):
        conductance = 0.5 * (own_vert + vert_z[lower:upper]) * open_z[lower:upper]
        summed = summed + conductance * (field_z[lower:upper] - center)
    return summed


def on_device(
    terminal, misfit, material, material_table, heater_slot, entry_heater, entry_block, profile
):
    time_step = 0.16
    layers, across, depth = terminal.shape
    steps = misfit.shape[0]
    width = 1
    matches = material[..., None] == jnp.arange(material_table.shape[1], dtype=jnp.int32)
    blocked = jnp.sum(
        jnp.where(matches[None], material_table[:, None, None, None, :], 0.0), axis=-1
    )
    blocked = extended_2(blocked, (("gx", 2),), width)
    cells = jnp.repeat(blocked, 128, axis=3)
    position = (
        lax.axis_index("gx") * across + jnp.arange(across + 2 * width, dtype=jnp.int32) - width
    )
    inside = (position >= 0) & (position < across * lax.axis_size("gx"))
    inside_x = inside.astype(jnp.float32)[None, :, None]
    accumulated = jnp.zeros_like(terminal)
    field = terminal
    for step_index in range(steps):
        extended = extended_2(field, (("gx", 1),), 1)
        field = (
            field + time_step * operate(extended, cells[0], cells[1], inside_x) + misfit[step_index]
        )
        accumulated = accumulated + field
    picked = accumulated.reshape(-1, 128)[entry_block]
    values = time_step * jnp.sum(picked * profile, axis=1)
    slots = heater_slot[entry_heater]
    dense = jnp.zeros((heater_slot.shape[0],), jnp.float32).at[slots].add(values)
    heater_grad = lax.psum_scatter(dense, "gx", scatter_dimension=0, tiled=True)
    return (field, heater_grad)


def solution(mesh):
    return jax.shard_map(
        on_device,
        mesh=mesh,
        in_specs=(
            P("groups", "gx", None),
            P(None, "groups", "gx", None),
            P(None, "gx", None),
            P(),
            P(),
            P("gx"),
            P("gx"),
            P("gx", None),
        ),
        out_specs=(P("groups", "gx", None), P(("groups", "gx"))),
        check_vma=False,
    )
```

profile of v0, /device:TPU:0, one launch (start us, length us, event | category | flops | bytes accessed | tf_op | source)
XLA Modules:
  0.0 170.2 jit_solution(14412996275298695265)
XLA Ops:
  0.6 0.0 copy-start
  0.6 0.9 iota_compare_fusion
  1.6 1.1 select_reduce_fusion
  2.7 2.4 %collective-permute-start = (f32[2,16,1,16]{3,2,1,0:T(1,128)S(1)}, f32[2,16,1,16]{3,2,1,0:T(1,128)S(1)}, u32[]{:S(2)}, u32[]{:S(2)}) collective-permute-start(f32[2,16,1,16]{3,2,1,0:T(1,128)S(1)} %get-tuple-element.31), channel_id=1, source_target_pairs={{0,1},{1,2},{2,3},{3,4},{4,5},{5,6},{6,7},{7,8},{8,9},{9,10},{10,1... | collective-permute-start | bytes 6152 | tf_op jit(solution)/shard_map/ppermute | solution.py:14
  5.1 1.3 collective-permute-start.1
  6.4 1.8 %copy.62 = f32[16,8,2048]{2,0,1:T(8,128)S(1)} copy(f32[16,8,2048]{2,1,0:T(8,128)} %param.8) | data formatting | bytes 2097152 | tf_op args[0]
  8.2 0.0 copy-start.9
  8.2 1.0 copy-done.9
  9.2 1.3 collective-permute-start.2
  10.5 5.8 %collective-permute-start.3 = (f32[16,1,2048]{2,0,1:T(8,128)S(1)}, f32[16,1,2048]{2,0,1:T(8,128)S(1)}, u32[]{:S(2)}, u32[]{:S(2)}) collective-permute-start(f32[16,1,2048]{2,0,1:T(8,128)S(1)} %get-tuple-element.28), channel_id=1, source_target_pairs={{0,1},{1,2},{2,3},{3,4},{4,5},{5,6},{6,7},{7,8},{8,9},{9,10},{10,1... | collective-permute-start | bytes 393224 | tf_op jit(solution)/shard_map/ppermute | solution.py:14
  16.3 4.3 %fusion.103 = (f32[1,16,8,2048]{3,2,1,0:T(8,128)}, f32[1,16,8,2048]{3,2,1,0:T(8,128)}, f32[1,16,8,2048]{3,2,1,0:T(8,128)}, f32[1,16,8,2048]{3,2,1,0:T(8,128)}) fusion(f32[4,16,8,2048]{3,2,1,0:T(8,128)} %param.9), kind=kLoop, calls=%fused_computation.151 | loop fusion | bytes 8388608 | tf_op jit(solution)/shard_map/slice | solution.py:68
  20.6 0.1 slice_multiply_fusion.1
  20.7 0.1 pad.55
  20.8 0.1 multiply_bitcast_fusion
  20.9 0.1 fusion.94
  21.0 0.0 collective-permute-done
  21.0 0.0 collective-permute-done.1
  21.0 0.1 pad_maximum_fusion.8
  21.1 0.4 broadcast_in_dim.47
  21.5 0.2 broadcast_in_dim.48
  21.7 0.0 copy-start.1
  21.8 0.4 broadcast_in_dim.49
  22.2 0.6 copy-done.1
  22.8 1.3 broadcast_in_dim.50
  24.1 1.4 slice.299
  25.5 0.0 collective-permute-done.2
  25.6 0.0 collective-permute-done.3
  25.6 0.4 slice-done
  25.9 5.8 %fusion.12 = (f32[16,8,2048]{2,0,1:T(8,128)S(1)}, f32[16,8,2048]{2,0,1:T(8,128)S(1)}, f32[16,8,2048]{2,0,1:T(8,128)S(1)}, f32[16,8,2048]{2,0,1:T(8,128)S(1)}, f3...) fusion(f32[16,8,2048]{2,0,1:T(8,128)S(1)} %copy-done.10, ...), kind=kLoop, calls=%fused_computation.35 | loop fusion | flops 8912896 | bytes 14958784 | tf_op jit(solution)/shard_map/add | solution.py:68
  31.8 1.0 copy-done.5
  32.7 0.7 fusion.106
  33.4 1.3 collective-permute-start.4
  34.7 4.3 %collective-permute-start.5 = (f32[16,1,2048]{2,0,1:T(8,128)}, f32[16,1,2048]{2,0,1:T(8,128)S(1)}, u32[]{:S(2)}, u32[]{:S(2)}) collective-permute-start(f32[16,1,2048]{2,0,1:T(8,128)} %get-tuple-element.26), channel_id=1, source_target_pairs={{0,1},{1,2},{2,3},{3,4},{4,5},{5,6},{6,7},{7,8},{8,9},{9,10},{10,1... | collective-permute-start | bytes 393224 | tf_op jit(solution)/shard_map/ppermute | solution.py:14
  39.0 11.8 %gather_fusion = s32[2048]{0:T(1024)S(1)} fusion(s32[8192]{0:T(1024)S(1)} %copy-done, s32[2048]{0:T(1024)S(1)} %fusion.92), kind=kCustom, calls=%fused_computation | custom fusion | bytes 24576 | tf_op jit(solution)/shard_map/gather | solution.py:73
  50.8 0.0 collective-permute-done.4
  50.8 0.0 collective-permute-done.5
  50.9 0.0 copy-start.16
  50.9 7.2 %fusion.23 = f32[16,8,2048]{2,0,1:T(8,128)S(1)} fusion(f32[16,8,2048]{2,0,1:T(8,128)} %copy-done.5, f32[16,8,2048]{2,0,1:T(8,128)} %get-tuple-element.16, f32[16,8,2048]{2,0,1:T(8,128)} %get-tuple-element.15, f32[16,8,2048]{2,0,1:T(8,128)} %get-tuple-element.14, f32[16,8,2048]{2,0,1:T(8,128)S(1)} %get-tuple-element.13, ...), kind=kLoop, calls=%fused_computation.46 | loop fusion | flops 5767168 | bytes 9699328 | tf_op jit(solution)/shard_map/add | solution.py:68
  58.1 1.0 copy-done.7
  59.1 0.7 fusion.105
  59.8 1.3 collective-permute-start.6
  61.1 4.3 %collective-permute-start.7 = (f32[16,1,2048]{2,0,1:T(8,128)}, f32[16,1,2048]{2,0,1:T(8,128)S(1)}, u32[]{:S(2)}, u32[]{:S(2)}) collective-permute-start(f32[16,1,2048]{2,0,1:T(8,128)} %get-tuple-element.24), channel_id=1, source_target_pairs={{0,1},{1,2},{2,3},{3,4},{4,5},{5,6},{6,7},{7,8},{8,9},{9,10},{10,1... | collective-permute-start | bytes 393224 | tf_op jit(solution)/shard_map/ppermute | solution.py:14
  65.4 0.6 dynamic-slice
  66.7 0.0 collective-permute-done.6
  66.7 0.0 collective-permute-done.7
  66.7 0.0 copy-start.15
  66.7 0.0 copy-start.2
  66.7 0.0 copy-start.3
  66.8 7.6 %fusion.34 = f32[16,8,2048]{2,0,1:T(8,128)S(1)} fusion(f32[16,8,2048]{2,0,1:T(8,128)} %copy-done.7, f32[16,8,2048]{2,0,1:T(8,128)} %get-tuple-element.16, f32[16,8,2048]{2,0,1:T(8,128)} %get-tuple-element.15, f32[16,8,2048]{2,0,1:T(8,128)} %get-tuple-element.14, f32[16,8,2048]{2,0,1:T(8,128)S(1)} %get-tuple-element.13, ...), kind=kLoop, calls=%fused_computation.57 | loop fusion | flops 5767168 | bytes 9699328 | tf_op jit(solution)/shard_map/add | solution.py:68
  74.4 1.3 collective-permute-start.8
  75.7 6.8 %collective-permute-start.9 = (f32[16,1,2048]{2,0,1:T(8,128)S(1)}, f32[16,1,2048]{2,0,1:T(8,128)S(1)}, u32[]{:S(2)}, u32[]{:S(2)}) collective-permute-start(f32[16,1,2048]{2,0,1:T(8,128)S(1)} %get-tuple-element.22), channel_id=1, source_target_pairs={{0,1},{1,2},{2,3},{3,4},{4,5},{5,6},{6,7},{7,8},{8,9},{9,10},{10,1... | collective-permute-start | bytes 393224 | tf_op jit(solution)/shard_map/ppermute | solution.py:14
  82.5 0.0 collective-permute-done.8
  82.5 0.7 collective-permute-done.9
  83.3 3.3 %add_add_fusion = (f32[16,8,2048]{2,0,1:T(8,128)S(1)}, f32[16,8,2048]{2,0,1:T(8,128)}) fusion(f32[16,8,2048]{2,0,1:T(8,128)S(1)} %fusion.34, f32[16,8,2048]{2,0,1:T(8,128)S(1)} %copy-done.6, f32[16,8,2048]{2,0,1:T(8,128)S(1)} %copy-done.8, f32[1,16,8,2048]{3,2,1,0:T(8,128)S(1)} %copy-done.12, f32[16,8,2048]{2,0,1:T(8,128)S(1)} %get-tuple-element.13, ...), kind=kLoop, calls=%fused_computation.128 | loop fusion | flops 6553600 | bytes 12845056 | tf_op jit(solution)/shard_map/add | solution.py:70
  86.6 0.6 copy.67
  87.2 0.2 reshape.70
  87.4 0.0 copy-start.13
  87.4 5.5 %gather_fusion.1 = f32[2048,128]{1,0:T(8,128)S(1)} fusion(f32[2048,128]{1,0:T(8,128)S(1)} %reshape.70, s32[2048]{0:T(1024)S(1)} %fusion.93), kind=kCustom, calls=%fused_computation.1 | custom fusion | bytes 2105344 | tf_op jit(solution)/shard_map/gather | solution.py:71
  92.9 0.0 copy-start.11
  92.9 0.3 multiply_reduce_fusion
  93.3 11.7 %scatter_custom_fusion = f32[8192]{0:T(1024)S(1)} fusion(s32[2048]{0:T(1024)S(1)} %bitcast.39, f32[2048]{0:T(1024)S(1)} %broadcast_multiply_fusion, f32[]{:T(128)} %constant.11.clone.1), kind=kCustom, calls=%fused_computation.137 | custom fusion | flops 2048 | bytes 32772 | tf_op jit(solution)/shard_map/scatter-add | solution.py:74
  105.0 63.0 %all-reduce.12 = f32[8192]{0:T(1024)S(1)} all-reduce(f32[8192]{0:T(1024)S(1)} %scatter_custom_fusion), channel_id=2, replica_groups=mesh['groups'=2,'gx'=16] {'gx'}, use_global_device_ids=true, to_apply=%region_3.4.clone | all-reduce | flops 8192 | bytes 65536
  168.0 1.6 copy.68
  169.6 0.7 dynamic-slice.1
  (37 shorter events, 0.2 us)
Async XLA Ops:
  0.6 38.4 %copy-start = (s32[8192]{0:T(1024)S(1)}, s32[8192]{0:T(1024)}, u32[]{:S(2)}) copy-start(s32[8192]{0:T(1024)} %param.12) | copy-start | bytes 98308
  2.7 18.3 %collective-permute-start = (f32[2,16,1,16]{3,2,1,0:T(1,128)S(1)}, f32[2,16,1,16]{3,2,1,0:T(1,128)S(1)}, u32[]{:S(2)}, u32[]{:S(2)}) collective-permute-start(f32[2,16,1,16]{3,2,1,0:T(1,128)S(1)} %get-tuple-element.31), channel_id=1, source_target_pairs={{0,1},{1,2},{2,3},{3,4},{4,5},{5,6},{6,7},{7,8},{8,9},{9,10},{10,1... | collective-permute-start | bytes 6152 | tf_op jit(solution)/shard_map/ppermute | solution.py:14
  5.1 15.9 %collective-permute-start.1 = (f32[2,16,1,16]{3,2,1,0:T(1,128)S(1)}, f32[2,16,1,16]{3,2,1,0:T(1,128)S(1)}, u32[]{:S(2)}, u32[]{:S(2)}) collective-permute-start(f32[2,16,1,16]{3,2,1,0:T(1,128)S(1)} %get-tuple-element.32), channel_id=1, source_target_pairs={{1,0},{2,1},{3,2},{4,3},{5,4},{6,5},{7,6},{8,7},{9,8},{10,9},{11,1... | collective-permute-start | bytes 6152 | tf_op jit(solution)/shard_map/ppermute | solution.py:15
  8.2 1.0 copy-start.9
  9.2 16.3 %collective-permute-start.2 = (f32[16,1,2048]{2,0,1:T(8,128)S(1)}, f32[16,1,2048]{2,0,1:T(8,128)S(1)}, u32[]{:S(2)}, u32[]{:S(2)}) collective-permute-start(f32[16,1,2048]{2,0,1:T(8,128)S(1)} %get-tuple-element.27), channel_id=1, source_target_pairs={{1,0},{2,1},{3,2},{4,3},{5,4},{6,5},{7,6},{8,7},{9,8},{10,9},{11,1... | collective-permute-start | bytes 393224 | tf_op jit(solution)/shard_map/ppermute | solution.py:15
  10.5 15.0 %collective-permute-start.3 = (f32[16,1,2048]{2,0,1:T(8,128)S(1)}, f32[16,1,2048]{2,0,1:T(8,128)S(1)}, u32[]{:S(2)}, u32[]{:S(2)}) collective-permute-start(f32[16,1,2048]{2,0,1:T(8,128)S(1)} %get-tuple-element.28), channel_id=1, source_target_pairs={{0,1},{1,2},{2,3},{3,4},{4,5},{5,6},{6,7},{7,8},{8,9},{9,10},{10,1... | collective-permute-start | bytes 393224 | tf_op jit(solution)/shard_map/ppermute | solution.py:14
  21.7 1.1 copy-start.1
  24.1 1.9 %slice-start = ((f32[16,10,2048]{2,0,1:T(8,128)}), f32[16,8,2048]{2,0,1:T(8,128)S(1)}, s32[]{:S(2)}) async-start(f32[16,10,2048]{2,0,1:T(8,128)} %copy-done.1), calls=%async_computation | async-start | bytes 2097152 | tf_op jit(solution)/shard_map/slice | solution.py:22
  24.1 1.9 %copy-start.10 = (f32[16,8,2048]{2,0,1:T(8,128)S(1)}, f32[16,8,2048]{2,0,1:T(8,128)}, u32[]{:S(2)}) copy-start(f32[16,8,2048]{2,0,1:T(8,128)} %copy-done.9) | copy-start | bytes 3145732
  25.9 13.1 %copy-start.14 = (s32[2048]{0:T(1024)S(1)}, s32[2048]{0:T(1024)}, u32[]{:S(2)}) copy-start(s32[2048]{0:T(1024)} %param.13) | copy-start | bytes 24580
  31.8 1.0 copy-start.5
  33.4 17.4 %collective-permute-start.4 = (f32[16,1,2048]{2,0,1:T(8,128)}, f32[16,1,2048]{2,0,1:T(8,128)S(1)}, u32[]{:S(2)}, u32[]{:S(2)}) collective-permute-start(f32[16,1,2048]{2,0,1:T(8,128)} %get-tuple-element.25), channel_id=1, source_target_pairs={{1,0},{2,1},{3,2},{4,3},{5,4},{6,5},{7,6},{8,7},{9,8},{10,9},{11,1... | collective-permute-start | bytes 393224 | tf_op jit(solution)/shard_map/ppermute | solution.py:15
  34.7 16.1 %collective-permute-start.5 = (f32[16,1,2048]{2,0,1:T(8,128)}, f32[16,1,2048]{2,0,1:T(8,128)S(1)}, u32[]{:S(2)}, u32[]{:S(2)}) collective-permute-start(f32[16,1,2048]{2,0,1:T(8,128)} %get-tuple-element.26), channel_id=1, source_target_pairs={{0,1},{1,2},{2,3},{3,4},{4,5},{5,6},{6,7},{7,8},{8,9},{9,10},{10,1... | collective-permute-start | bytes 393224 | tf_op jit(solution)/shard_map/ppermute | solution.py:14
  50.9 14.6 %copy-start.16 = (u32[32]{0:T(128)S(1)}, u32[32]{0:T(128)}, u32[]{:S(2)}) copy-start(u32[32]{0:T(128)} %constant.60) | copy-start | bytes 388
  58.1 1.0 copy-start.7
  59.8 6.8 %collective-permute-start.6 = (f32[16,1,2048]{2,0,1:T(8,128)}, f32[16,1,2048]{2,0,1:T(8,128)S(1)}, u32[]{:S(2)}, u32[]{:S(2)}) collective-permute-start(f32[16,1,2048]{2,0,1:T(8,128)} %get-tuple-element.23), channel_id=1, source_target_pairs={{1,0},{2,1},{3,2},{4,3},{5,4},{6,5},{7,6},{8,7},{9,8},{10,9},{11,1... | collective-permute-start | bytes 393224 | tf_op jit(solution)/shard_map/ppermute | solution.py:15
  61.1 5.6 %collective-permute-start.7 = (f32[16,1,2048]{2,0,1:T(8,128)}, f32[16,1,2048]{2,0,1:T(8,128)S(1)}, u32[]{:S(2)}, u32[]{:S(2)}) collective-permute-start(f32[16,1,2048]{2,0,1:T(8,128)} %get-tuple-element.24), channel_id=1, source_target_pairs={{0,1},{1,2},{2,3},{3,4},{4,5},{5,6},{6,7},{7,8},{8,9},{9,10},{10,1... | collective-permute-start | bytes 393224 | tf_op jit(solution)/shard_map/ppermute | solution.py:14
  66.7 15.8 %copy-start.15 = (s32[2048]{0:T(1024)S(1)}, s32[2048]{0:T(1024)}, u32[]{:S(2)}) copy-start(s32[2048]{0:T(1024)} %param.14) | copy-start | bytes 24580
  66.7 16.5 %copy-start.2 = (f32[16,8,2048]{2,0,1:T(8,128)S(1)}, f32[16,8,2048]{2,0,1:T(8,128)}, u32[]{:S(2)}) copy-start(f32[16,8,2048]{2,0,1:T(8,128)} %get-tuple-element.14) | copy-start | bytes 3145732
  66.7 16.5 %copy-start.3 = (f32[16,8,2048]{2,0,1:T(8,128)S(1)}, f32[16,8,2048]{2,0,1:T(8,128)}, u32[]{:S(2)}) copy-start(f32[16,8,2048]{2,0,1:T(8,128)} %get-tuple-element.15) | copy-start | bytes 3145732
  66.7 16.5 %copy-start.4 = (f32[16,8,2048]{2,0,1:T(8,128)S(1)}, f32[16,8,2048]{2,0,1:T(8,128)}, u32[]{:S(2)}) copy-start(f32[16,8,2048]{2,0,1:T(8,128)} %get-tuple-element.16) | copy-start | bytes 3145732
  66.7 16.5 %copy-start.6 = (f32[16,8,2048]{2,0,1:T(8,128)S(1)}, f32[16,8,2048]{2,0,1:T(8,128)}, u32[]{:S(2)}) copy-start(f32[16,8,2048]{2,0,1:T(8,128)} %copy-done.5) | copy-start | bytes 3145732
  66.7 16.5 %copy-start.8 = (f32[16,8,2048]{2,0,1:T(8,128)S(1)}, f32[16,8,2048]{2,0,1:T(8,128)}, u32[]{:S(2)}) copy-start(f32[16,8,2048]{2,0,1:T(8,128)} %copy-done.7) | copy-start | bytes 3145732
  66.8 16.5 %copy-start.12 = (f32[1,16,8,2048]{3,2,1,0:T(8,128)S(1)}, f32[1,16,8,2048]{3,2,1,0:T(8,128)}, u32[]{:S(2)}) copy-start(f32[1,16,8,2048]{3,2,1,0:T(8,128)} %get-tuple-element.17) | copy-start | bytes 3145732
  74.4 8.1 %collective-permute-start.8 = (f32[16,1,2048]{2,0,1:T(8,128)S(1)}, f32[16,1,2048]{2,0,1:T(8,128)S(1)}, u32[]{:S(2)}, u32[]{:S(2)}) collective-permute-start(f32[16,1,2048]{2,0,1:T(8,128)S(1)} %get-tuple-element.21), channel_id=1, source_target_pairs={{1,0},{2,1},{3,2},{4,3},{5,4},{6,5},{7,6},{8,7},{9,8},{10,9},{11,1... | collective-permute-start | bytes 393224 | tf_op jit(solution)/shard_map/ppermute | solution.py:15
  75.7 7.6 %collective-permute-start.9 = (f32[16,1,2048]{2,0,1:T(8,128)S(1)}, f32[16,1,2048]{2,0,1:T(8,128)S(1)}, u32[]{:S(2)}, u32[]{:S(2)}) collective-permute-start(f32[16,1,2048]{2,0,1:T(8,128)S(1)} %get-tuple-element.22), channel_id=1, source_target_pairs={{0,1},{1,2},{2,3},{3,4},{4,5},{5,6},{6,7},{7,8},{8,9},{9,10},{10,1... | collective-permute-start | bytes 393224 | tf_op jit(solution)/shard_map/ppermute | solution.py:14
  87.4 5.5 %copy-start.13 = (f32[2048,128]{1,0:T(8,128)S(1)}, f32[2048,128]{1,0:T(8,128)}, u32[]{:S(2)}) copy-start(f32[2048,128]{1,0:T(8,128)} %param.15) | copy-start | bytes 3145732
  92.9 75.1 %copy-start.11 = (f32[16,8,2048]{2,0,1:T(8,128)S(1)}, f32[16,8,2048]{2,0,1:T(8,128)}, u32[]{:S(2)}) copy-start(f32[16,8,2048]{2,0,1:T(8,128)} %get-tuple-element.9) | copy-start | bytes 3145732
where the time goes:
time: 171 us; the launch traced here: 170 us
  blocking collectives  63 us (37%)
  other arithmetic  38.4 us (22%)
  local copies, waits for them, and re-layouts  36.4 us (21%)
  starting transfers between devices  29.9 us (17%)
  between operations  1.78 us (1%)
    unnamed x1, blocking collectives  63 us
    ppermute x5, starting transfers between devices, extended_2(): before = lax.ppermute(last, axis, up)  23.5 us
    add x3, other arithmetic, on_device(): field + time_step * operate(extended, cells[0], cells[1], inside_x)  20.6 us
    gather x1, local copies, waits for them, and re-layouts, on_device(): slots = heater_slot[entry_heater]  11.8 us
    scatter-add x1, other arithmetic, on_device(): jnp.zeros((heater_slot.shape[0],), jnp.float32).at[slots].add(values)  11.7 us
    unnamed x38, local copies, waits for them, and re-layouts  8.29 us
    ppermute x5, starting transfers between devices, extended_2(): after = lax.ppermute(leading, axis, down)  6.44 us
    gather x1, local copies, waits for them, and re-layouts, on_device(): picked = accumulated.reshape(-1, 128)[entry_block]  5.47 us
  transfers between devices with their start and end apart: 10, of which 1 were waited for; matrix products, arithmetic and copies ran while one was open for 13% of the time, Pallas kernels for 0%

commit v1 on v0

v1 whole, which is shorter than its diff:
```python
import functools

import jax
import jax.numpy as jnp
from jax import lax
from jax.experimental import pallas as pl
from jax.experimental.pallas import tpu as pltpu
from jax.sharding import PartitionSpec as P

MESH = pl.DeviceIdType.MESH
DT = 0.16
LANES = 128


def ceil8(rows):
    return (rows + 7) // 8 * 8


def kernel(
    n, layers, across, nyb, steps, mats, per_owner,
    term, misfit, mat, table, slot_table, heaters, block, profile,
    adjoint, grad,
    fields, mis, prof, gxp, gxm, gyp, gym, gz, c0, packed, vpacked, total, picked,
    one_lo, one_hi, dense, send_lo, send_hi, from_lo, from_hi, parts,
    sem_term, sem_mis, sem_prof, sem_out, send_sems, recv_sems, out_sems, in_sems,
):
    me = lax.axis_index("gx")
    slab = nyb * across
    rows = layers * slab
    edge = nyb * layers
    table_rows = slot_table.shape[0]
    entries = heaters.shape[0] * LANES
    owner_rows = per_owner // LANES
    pad_rows = ceil8(owner_rows)

    barrier = pltpu.get_barrier_semaphore()

    def greet(d, _):
        pl.semaphore_signal(
            barrier, inc=1, device_id={"gx": lax.rem(me + d, n)}, device_id_type=MESH
        )
        return 0

    lax.fori_loop(1, n, greet, 0)

    load_term = pltpu.make_async_copy(term, fields.at[0, pl.ds(slab, rows)], sem_term)
    load_term.start()
    loads = [
        pltpu.make_async_copy(misfit.at[t], mis.at[t], sem_mis.at[t]) for t in range(steps)
    ]
    for load in loads:
        load.start()
    load_prof = pltpu.make_async_copy(profile, prof, sem_prof)
    load_prof.start()

    sub = lax.broadcasted_iota(jnp.int32, (across, LANES), 0)
    lane = lax.broadcasted_iota(jnp.int32, (across, LANES), 1)
    lane_e = lax.broadcasted_iota(jnp.int32, (layers, LANES), 1)

    index = mat[...]
    lat = jnp.zeros(index.shape, jnp.float32)
    ver = jnp.zeros(index.shape, jnp.float32)
    for m in range(mats):
        lat = jnp.where(index == m, table[0, m], lat)
        ver = jnp.where(index == m, table[1, m], ver)
    packed[...] = jnp.zeros(packed.shape, jnp.float32)
    vpacked[...] = jnp.zeros(vpacked.shape, jnp.float32)
    packed[:, pl.ds(0, nyb)] = lat
    vpacked[:, pl.ds(0, nyb)] = ver

    zeros_slab = jnp.zeros((slab, LANES), jnp.float32)
    for t in range(steps):
        fields[t, pl.ds(0, slab), :] = zeros_slab
        fields[t, pl.ds(slab + rows, slab), :] = zeros_slab
    gz[pl.ds(0, slab), :] = zeros_slab
    gz[pl.ds(rows, slab), :] = zeros_slab

    @pl.when(me == 0)
    def _():
        from_lo[...] = jnp.zeros(from_lo.shape, jnp.float32)

    @pl.when(me == n - 1)
    def _():
        from_hi[...] = jnp.zeros(from_hi.shape, jnp.float32)

    def hop(t, up):
        count = edge + layers if t == 0 else edge
        s = 1 if up else 0
        return pltpu.make_async_remote_copy(
            src_ref=(send_hi if up else send_lo).at[t, pl.ds(0, count)],
            dst_ref=(from_lo if up else from_hi).at[t, pl.ds(0, count)],
            send_sem=send_sems.at[t, s],
            recv_sem=recv_sems.at[t, s],
            device_id={"gx": me + 1 if up else me - 1},
            device_id_type=MESH,
        )

    def send(t):
        @pl.when(me < n - 1)
        def _():
            hop(t, True).start()

        @pl.when(me > 0)
        def _():
            hop(t, False).start()

    def receive(t):
        @pl.when(me > 0)
        def _():
            hop(t, True).wait_recv()

        @pl.when(me < n - 1)
        def _():
            hop(t, False).wait_recv()

    load_term.wait()
    for s, (buffer, x) in enumerate(((send_lo, 0), (send_hi, across - 1))):
        for b in range(nyb):
            buffer[0, pl.ds(b * layers, layers), :] = fields[
                0, pl.ds(slab + b * across + x, layers, stride=slab), :
            ]
        buffer[0, pl.ds(edge, layers), :] = packed[pl.ds(x, layers, stride=across), :]
    pl.semaphore_wait(barrier, n - 1)
    send(0)

    half = 0.5 * DT

    def coefficients(k, _):
        at = pl.multiple_of(k * across, across)
        base = pl.multiple_of(k * slab, slab)
        lat = packed[pl.ds(at, across), :]
        ver = vpacked[pl.ds(at, across), :]
        upper = jnp.minimum(k + 1, layers - 1)
        ver_up = vpacked[pl.ds(pl.multiple_of(upper * across, across), across), :]
        lower = jnp.maximum(k - 1, 0)
        ver_down = vpacked[pl.ds(pl.multiple_of(lower * across, across), across), :]
        z_up = jnp.where(k < layers - 1, half, 0.0) * (ver + ver_up)
        z_down = jnp.where(k > 0, half, 0.0) * (ver + ver_down)
        x_up = half * (lat + pltpu.roll(lat, across - 1, 0))
        x_down = half * (lat + pltpu.roll(lat, 1, 0))
        side = half * (lat + pltpu.roll(lat, LANES - 1, 1))
        inner = DT * lat
        center = 1.0 - z_up - z_down

        def wide(value, b):
            return jnp.broadcast_to(value[:, b : b + 1], (across, LANES))

        none = jnp.zeros((across, LANES), jnp.float32)
        sides = [none] + [wide(side, b) for b in range(nyb - 1)] + [none]
        for b in range(nyb):
            own = pl.ds(base + b * across, across)
            y = wide(inner, b)
            y_up = jnp.where(lane == LANES - 1, sides[b + 1], y)
            y_down = jnp.where(lane == 0, sides[b], y)
            gyp[own, :] = y_up
            gym[own, :] = y_down
            gxp[own, :] = wide(x_up, b)
            gxm[own, :] = wide(x_down, b)
            gz[pl.ds(base + slab + b * across, across), :] = wide(z_up, b)
            c0[own, :] = wide(center, b) - y_up - y_down
        return 0

    lax.fori_loop(0, layers, coefficients, 0)

    cut = 4
    width = cut * LANES
    slots = slot_table[...]
    pieces = jnp.concatenate(
        [
            jnp.right_shift(slots, 8).astype(jnp.float32).T,
            jnp.bitwise_and(slots, 255).astype(jnp.float32).T,
        ],
        axis=0,
    ).astype(jnp.bfloat16)

    def lookup(c, _):
        heater = jnp.concatenate(
            [heaters[pl.ds(c * cut + j, 1), :] for j in range(cut)], axis=1
        )
        high = (
            lax.broadcasted_iota(jnp.int32, (table_rows, width), 0)
            == jnp.right_shift(heater, 7)
        ).astype(jnp.float32).astype(jnp.bfloat16)
        found = jnp.dot(pieces, high, preferred_element_type=jnp.float32)
        lanes = lax.broadcasted_iota(jnp.int32, (LANES, width), 0)
        mine = lanes == jnp.bitwise_and(heater, LANES - 1)
        big = jnp.sum(jnp.where(mine, found[:LANES], 0.0), axis=0, keepdims=True)
        small = jnp.sum(jnp.where(mine, found[LANES:], 0.0), axis=0, keepdims=True)
        slot = (big * 256.0 + small).astype(jnp.int32)
        owner = slot // per_owner
        place = owner * pad_rows + (slot - owner * per_owner) // LANES
        one_hi[:, pl.ds(pl.multiple_of(c * width, width), width)] = (
            lax.broadcasted_iota(jnp.int32, (n * pad_rows, width), 0) == place
        ).astype(jnp.float32).astype(jnp.bfloat16)
        low = (lanes == jnp.bitwise_and(slot, LANES - 1)).astype(jnp.float32)
        for j in range(cut):
            one_lo[pl.ds(pl.multiple_of(c * width, width) + j * LANES, LANES), :] = low[
                :, j * LANES : (j + 1) * LANES
            ].T
        return 0

    lookups = entries // width
    lax.fori_loop(0, lookups, lookup, 0)

    receive(0)
    for x, ref, arrived, outside in (
        (0, gxm, from_lo, me == 0),
        (across - 1, gxp, from_hi, me == n - 1),
    ):
        scale = jnp.where(outside, 0.0, half)
        pair = scale * (
            packed[pl.ds(x, layers, stride=across), :] + arrived[0, pl.ds(edge, layers), :]
        )
        for b in range(nyb):
            ref[pl.ds(b * across + x, layers, stride=slab), :] = jnp.broadcast_to(
                pair[:, b : b + 1], (layers, LANES)
            )

    def edges(t):
        for x, inward, g_in, g_out, arrived, buffer in (
            (0, 1, gxp, gxm, from_lo, send_lo),
            (across - 1, -1, gxm, gxp, from_hi, send_hi),
        ):
            def at(ref, b, shift=0):
                return ref[pl.ds(shift + b * across + x, layers, stride=slab), :]

            def at_f(b, shift):
                return fields[t, pl.ds(shift + b * across + x, layers, stride=slab), :]

            v = [at_f(b, slab) for b in range(nyb)]
            right = [pltpu.roll(u, LANES - 1, 1) for u in v]
            left = [pltpu.roll(u, 1, 1) for u in v]
            for b in range(nyb):
                y_up = jnp.where(lane_e == LANES - 1, right[min(b + 1, nyb - 1)], right[b])
                y_down = jnp.where(lane_e == 0, left[max(b - 1, 0)], left[b])
                here = v[b]
                inner = at_f(b, slab + inward)
                outer = arrived[t, pl.ds(b * layers, layers), :]
                new = (
                    (at(c0, b) * here + at(gyp, b) * y_up)
                    + (at(gym, b) * y_down + at(g_in, b) * (inner - here))
                ) + (
                    (at(g_out, b) * (outer - here) + at(gz, b, slab) * at_f(b, 2 * slab))
                    + (at(gz, b) * at_f(b, 0)
                       + mis[t, pl.ds(b * across + x, layers, stride=slab), :])
                )
                buffer[t + 1, pl.ds(b * layers, layers), :] = new

    def interior(t, last):
        def body(k, _):
            base = pl.multiple_of(k * slab, slab)
            v = [fields[t, pl.ds(base + slab + b * across, across), :] for b in range(nyb)]
            right = [pltpu.roll(u, LANES - 1, 1) for u in v]
            left = [pltpu.roll(u, 1, 1) for u in v]
            for b in range(nyb):
                own = pl.ds(base + b * across, across)
                here = v[b]
                y_up = jnp.where(lane == LANES - 1, right[min(b + 1, nyb - 1)], right[b])
                y_down = jnp.where(lane == 0, left[max(b - 1, 0)], left[b])
                x_up = jnp.where(
                    sub == across - 1,
                    from_hi[t, pl.ds(b * layers + k, 1), :],
                    pltpu.roll(here, across - 1, 0),
                )
                x_down = jnp.where(
                    sub == 0, from_lo[t, pl.ds(b * layers + k, 1), :], pltpu.roll(here, 1, 0)
                )
                z_up = fields[t, pl.ds(base + 2 * slab + b * across, across), :]
                z_down = fields[t, own, :]
                new = (
                    (c0[own, :] * here + gyp[own, :] * y_up)
                    + (gym[own, :] * y_down + gxp[own, :] * (x_up - here))
                ) + (
                    (gxm[own, :] * (x_down - here)
                     + gz[pl.ds(base + slab + b * across, across), :] * z_up)
                    + (gz[own, :] * z_down + mis[t, own, :])
                )
                if last:
                    picked[own, :] = new
                    acc = new
                    for s in range(1, steps):
                        acc = acc + fields[s, pl.ds(base + slab + b * across, across), :]
                    total[pl.ds(base + b, across, stride=nyb), :] = acc
                else:
                    fields[t + 1, pl.ds(base + slab + b * across, across), :] = new
            return 0

        lax.fori_loop(0, layers, body, 0)

    for t in range(steps):
        last = t == steps - 1
        loads[t].wait()
        if t > 0:
            receive(t)
        if not last:
            edges(t)
            send(t + 1)
        interior(t, last)

    store = pltpu.make_async_copy(picked.at[pl.ds(0, rows)], adjoint, sem_out)
    store.start()
    load_prof.wait()

    unroll = 32

    def pick(c, _):
        base = pl.multiple_of(c * unroll, unroll)
        for j in range(unroll):
            picked[pl.ds(rows + base + j, 1), :] = total[pl.ds(block[base + j], 1), :]
        return 0

    lax.fori_loop(0, entries // unroll, pick, 0)

    chunk = 512
    sums = jnp.zeros((n * pad_rows, 3 * LANES), jnp.float32)
    for c in range(entries // chunk):
        own = pl.ds(c * chunk, chunk)
        value = DT * jnp.sum(
            picked[pl.ds(rows + c * chunk, chunk), :] * prof[own, :], axis=1, keepdims=True
        )
        spread = one_lo[own, :] * value
        first = spread.astype(jnp.bfloat16)
        rest = spread - first.astype(jnp.float32)
        second = rest.astype(jnp.bfloat16)
        third = (rest - second.astype(jnp.float32)).astype(jnp.bfloat16)
        sums = sums + jnp.dot(
            one_hi[:, c * chunk : (c + 1) * chunk],
            jnp.concatenate([first, second, third], axis=1),
            preferred_element_type=jnp.float32,
        )
    dense[...] = (
        (sums[:, 2 * LANES :] + sums[:, LANES : 2 * LANES]) + sums[:, :LANES]
    ).reshape(n, pad_rows, LANES)

    def deliver(d):
        peer = lax.rem(me + d, n)
        return pltpu.make_async_remote_copy(
            src_ref=dense.at[peer],
            dst_ref=parts.at[d],
            send_sem=out_sems.at[d],
            recv_sem=in_sems.at[d],
            device_id={"gx": peer},
            device_id_type=MESH,
        )

    def start(d, _):
        deliver(d).start()
        return 0

    lax.fori_loop(1, n, start, 0)

    for t in range(steps):
        @pl.when(me < n - 1)
        def _():
            hop(t, True).wait_send()

        @pl.when(me > 0)
        def _():
            hop(t, False).wait_send()

    store.wait()

    def finish(d, acc):
        deliver(d).wait_recv()
        return acc + parts[d]

    result = lax.fori_loop(1, n, finish, dense[me])
    grad[...] = result[:owner_rows]

    def drain(d, _):
        deliver(d).wait_send()
        return 0

    lax.fori_loop(1, n, drain, 0)


def on_device(
    terminal, misfit, material, material_table, heater_slot, entry_heater, entry_block, profile
):
    n = lax.axis_size("gx")
    layers, across, depth = terminal.shape
    steps = misfit.shape[0]
    mats = material_table.shape[1]
    nyb = depth // LANES
    entries = entry_block.shape[0]
    per_owner = heater_slot.shape[0] // n
    rows, slab, edge = layers * across * nyb, across * nyb, layers * nyb
    pad_rows = ceil8(per_owner // LANES)
    term = terminal.reshape(layers, across, nyb, LANES).swapaxes(1, 2).reshape(rows, LANES)
    mis = (
        misfit.reshape(steps, layers, across, nyb, LANES).swapaxes(2, 3).reshape(steps, rows, LANES)
    )
    any_space = pl.BlockSpec(memory_space=pl.ANY)
    vmem = pl.BlockSpec(memory_space=pltpu.VMEM)
    smem = pl.BlockSpec(memory_space=pltpu.SMEM)
    f32 = jnp.float32
    adjoint, grad = pl.pallas_call(
        functools.partial(kernel, n, layers, across, nyb, steps, mats, per_owner),
        out_shape=(
            jax.ShapeDtypeStruct((rows, LANES), f32),
            jax.ShapeDtypeStruct((per_owner // LANES, LANES), f32),
        ),
        in_specs=[any_space, any_space, vmem, smem, vmem, vmem, smem, any_space],
        out_specs=(any_space, vmem),
        scratch_shapes=[
            pltpu.VMEM((steps, rows + 2 * slab, LANES), f32),
            pltpu.VMEM((steps, rows, LANES), f32),
            pltpu.VMEM((entries, LANES), f32),
            pltpu.VMEM((rows, LANES), f32),
            pltpu.VMEM((rows, LANES), f32),
            pltpu.VMEM((rows, LANES), f32),
            pltpu.VMEM((rows, LANES), f32),
            pltpu.VMEM((rows + slab, LANES), f32),
            pltpu.VMEM((rows, LANES), f32),
            pltpu.VMEM((layers * across, LANES), f32),
            pltpu.VMEM((layers * across, LANES), f32),
            pltpu.VMEM((rows, LANES), f32),
            pltpu.VMEM((rows + entries, LANES), f32),
            pltpu.VMEM((entries, LANES), f32),
            pltpu.VMEM((n * pad_rows, entries), jnp.bfloat16),
            pltpu.VMEM((n, pad_rows, LANES), f32),
            pltpu.VMEM((steps, edge + layers, LANES), f32),
            pltpu.VMEM((steps, edge + layers, LANES), f32),
            pltpu.VMEM((steps, edge + layers, LANES), f32),
            pltpu.VMEM((steps, edge + layers, LANES), f32),
            pltpu.VMEM((n, pad_rows, LANES), f32),
            pltpu.SemaphoreType.DMA,
            pltpu.SemaphoreType.DMA((steps,)),
            pltpu.SemaphoreType.DMA,
            pltpu.SemaphoreType.DMA,
            pltpu.SemaphoreType.DMA((steps, 2)),
            pltpu.SemaphoreType.DMA((steps, 2)),
            pltpu.SemaphoreType.DMA((n,)),
            pltpu.SemaphoreType.DMA((n,)),
        ],
        compiler_params=pltpu.CompilerParams(
            collective_id=0, has_side_effects=True, vmem_limit_bytes=48 * 1024 * 1024
        ),
    )(
        term,
        mis,
        material.reshape(layers * across, nyb),
        material_table,
        heater_slot.reshape(-1, LANES),
        entry_heater.reshape(-1, LANES),
        entry_block,
        profile,
    )
    adjoint = adjoint.reshape(layers, nyb, across, LANES).swapaxes(1, 2).reshape(terminal.shape)
    return (adjoint, grad.reshape(per_owner))


def solution(mesh):
    return jax.shard_map(
        on_device,
        mesh=mesh,
        in_specs=(
            P("groups", "gx", None),
            P(None, "groups", "gx", None),
            P(None, "gx", None),
            P(),
            P(),
            P("gx"),
            P("gx"),
            P("gx", None),
        ),
        out_specs=(P("groups", "gx", None), P(("groups", "gx"))),
        check_vma=False,
    )
```

time: 171 us -> 50.2 us (0.29)
  blocking collectives: 63 us -> 0 us
  Pallas kernels: 0 us -> 41.5 us
  other arithmetic: 38.4 us -> 0 us
  starting transfers between devices: 29.9 us -> 0 us
  local copies, waits for them, and re-layouts: 36.4 us -> 7.66 us
    unnamed x1 -> x0, blocking collectives: 63 us -> none
    pallas_call x0 -> x1, Pallas kernels: none -> 41.5 us  [on_device(): pl.pallas_call(functools.partial(kernel, n, layers, across, nyb, steps, m...]
    ppermute x10 -> x0, starting transfers between devices: 29.9 us -> none  [the longest x5 23.5 us: extended_2(): before = lax.ppermute(last, axis, up)]
    add x4 -> x0, other arithmetic: 24 us -> none  [the longest x3 20.6 us: on_device(): field + time_step * operate(extended, cells[0], cells[1], inside_x)]
    gather x2 -> x0, local copies, waits for them, and re-layouts: 17.2 us -> none  [the longest x1 11.8 us: on_device(): slots = heater_slot[entry_heater]]
    scatter-add x1 -> x0, other arithmetic: 11.7 us -> none  [on_device(): jnp.zeros((heater_slot.shape[0],), jnp.float32).at[slots].add(values)]
    slice x12 -> x0, local copies, waits for them, and re-layouts: 7.69 us -> none  [the longest x1 4.3 us: on_device(): misfit[step_index]]
    broadcast_in_dim x4 -> x0, local copies, waits for them, and re-layouts: 2.27 us -> none  [on_device(): cells = jnp.repeat(blocked, 128, axis=3)]
  transfers between devices with their start and end apart: 10 -> 0, of which waited for: 1 -> 0; matrix products, arithmetic and copies ran while one was open for 13% -> 0% of each run, Pallas kernels for 0% -> 0%
where the time goes in v1:
time: 50.2 us; the launch traced here: 49.8 us
  Pallas kernels  41.5 us (83%)
  local copies, waits for them, and re-layouts  7.66 us (15%)
  between operations  0.66 us (1%)
    pallas_call x1, Pallas kernels, on_device(): pl.pallas_call(functools.partial(kernel, n, layers, across, nyb, steps, m...  41.5 us
    unnamed x16, local copies, waits for them, and re-layouts  7.66 us

profile of v1, /device:TPU:0, one launch (start us, length us, event | category | flops | bytes accessed | tf_op | source)
XLA Modules:
  0.0 49.8 jit_solution(653267467877950263)
XLA Ops:
  0.6 0.0 copy-start
  0.6 1.2 %copy-done = f32[16,8,2048]{2,1,0:T(8,128)S(1)} copy-done((f32[16,8,2048]{2,1,0:T(8,128)S(1)}, f32[16,8,2048]{2,1,0:T(8,128)}, u32[]{:S(2)}) %copy-start) | copy-done | bytes 1048600
  1.9 0.0 copy-start.1
  1.9 1.2 %copy-done.1 = f32[2048,128]{1,0:T(8,128)S(1)} copy-done((f32[2048,128]{1,0:T(8,128)S(1)}, f32[2048,128]{1,0:T(8,128)}, u32[]{:S(2)}) %copy-start.1) | copy-done | bytes 1048600
  3.1 0.0 copy-start.2
  3.1 0.8 %copy-done.2 = s32[16,8,16]{2,1,0:T(8,128)S(1)} copy-done((s32[16,8,16]{2,1,0:T(8,128)S(1)}, s32[16,8,16]{2,1,0:T(8,128)}, u32[]{:S(2)}) %copy-start.2) | copy-done | bytes 8216
  3.9 0.0 copy-start.3
  3.9 0.8 %copy-done.3 = s32[8192]{0:T(1024)S(1)} copy-done((s32[8192]{0:T(1024)S(1)}, s32[8192]{0:T(1024)}, u32[]{:S(2)}) %copy-start.3) | copy-done | bytes 32792
  4.7 0.0 copy-start.4
  4.7 0.7 %copy-done.4 = s32[2048]{0:T(1024)S(1)} copy-done((s32[2048]{0:T(1024)S(1)}, s32[2048]{0:T(1024)}, u32[]{:S(2)}) %copy-start.4) | copy-done | bytes 8216
  5.4 0.0 copy-start.5
  5.4 0.7 %copy-done.5 = s32[2048]{0:T(1024)S(1)} copy-done((s32[2048]{0:T(1024)S(1)}, s32[2048]{0:T(1024)}, u32[]{:S(2)}) %copy-start.5) | copy-done | bytes 8216
  6.1 0.0 copy-start.6
  6.1 0.7 %copy-done.6 = f32[2,8]{1,0:T(2,128)S(1)} copy-done((f32[2,8]{1,0:T(2,128)S(1)}, f32[2,8]{1,0:T(2,128)}, u32[]{:S(2)}) %copy-start.6) | copy-done | bytes 88
  6.8 41.5 %shard_map.95 = (f32[2048,128]{1,0:T(8,128)S(1)}, f32[4,128]{1,0:T(4,128)S(1)}) custom-call(f32[2048,128]{1,0:T(8,128)S(1)} %bitcast.20, f32[4,2048,128]{2,1,0:T(8,128)} %bitcast.25, s32[128,16]{1,0:T(8,128)S(1)} %bitcast.21, f32[2,8]{1,0:T(2,128)S(1)} %copy-done.6, s32[64,128]{1,0:T(8,128)S(1)} %bitcast.22, s32[16,128]{1,0:T(8,128)S(1)} %bitcast.23, ...), custom_call_target="tpu_custom_call" | custom-call | tf_op jit(solution)/shard_map/pallas_call | solution.py:397
  48.3 1.0 %copy.12 = f32[16,8,2048]{2,1,0:T(8,128)} copy(f32[16,8,2048]{2,1,0:T(8,128)S(1)} %bitcast.19) | data formatting | bytes 2097152
  49.2 0.6 %copy.13 = f32[512]{0:T(512)} copy(f32[512]{0:T(512)S(1)} %bitcast.24) | data formatting | bytes 4096
Async XLA Ops:
  0.6 1.2 %copy-start = (f32[16,8,2048]{2,1,0:T(8,128)S(1)}, f32[16,8,2048]{2,1,0:T(8,128)}, u32[]{:S(2)}) copy-start(f32[16,8,2048]{2,1,0:T(8,128)} %param.8) | copy-start | bytes 3145732
  1.9 1.2 %copy-start.1 = (f32[2048,128]{1,0:T(8,128)S(1)}, f32[2048,128]{1,0:T(8,128)}, u32[]{:S(2)}) copy-start(f32[2048,128]{1,0:T(8,128)} %profile.1) | copy-start | bytes 3145732
  3.1 0.8 %copy-start.2 = (s32[16,8,16]{2,1,0:T(8,128)S(1)}, s32[16,8,16]{2,1,0:T(8,128)}, u32[]{:S(2)}) copy-start(s32[16,8,16]{2,1,0:T(8,128)} %param.10) | copy-start | bytes 24580
  3.9 0.8 %copy-start.3 = (s32[8192]{0:T(1024)S(1)}, s32[8192]{0:T(1024)}, u32[]{:S(2)}) copy-start(s32[8192]{0:T(1024)} %param.12) | copy-start | bytes 98308
  4.7 0.7 %copy-start.4 = (s32[2048]{0:T(1024)S(1)}, s32[2048]{0:T(1024)}, u32[]{:S(2)}) copy-start(s32[2048]{0:T(1024)} %param.13) | copy-start | bytes 24580
  5.4 0.7 %copy-start.5 = (s32[2048]{0:T(1024)S(1)}, s32[2048]{0:T(1024)}, u32[]{:S(2)}) copy-start(s32[2048]{0:T(1024)} %block.1) | copy-start | bytes 24580
  6.1 0.7 %copy-start.6 = (f32[2,8]{1,0:T(2,128)S(1)}, f32[2,8]{1,0:T(2,128)}, u32[]{:S(2)}) copy-start(f32[2,8]{1,0:T(2,128)} %table.1) | copy-start | bytes 196

commit v2 on v1

--- a/solution.py
+++ b/solution.py
@@ -18,11 +18,12 @@
 
 def kernel(
     n, layers, across, nyb, steps, mats, per_owner,
-    term, misfit, mat, table, slot_table, heaters, block, profile,
+    term, misfit, mat_hbm, table_hbm, slots_hbm, heaters_hbm, block_hbm, profile,
     adjoint, grad,
+    mat, table, slot_table, heaters, block,
     fields, mis, prof, gxp, gxm, gyp, gym, gz, c0, packed, vpacked, total, picked,
     one_lo, one_hi, dense, send_lo, send_hi, from_lo, from_hi, parts,
-    sem_term, sem_mis, sem_prof, sem_out, send_sems, recv_sems, out_sems, in_sems,
+    sem_term, sem_mis, sem_prof, sem_small, send_sems, recv_sems, out_sems, in_sems,
 ):
     me = lax.axis_index("gx")
     slab = nyb * across
@@ -43,6 +44,15 @@
 
     lax.fori_loop(1, n, greet, 0)
 
+    small = [
+        pltpu.make_async_copy(source, target, sem_small.at[i])
+        for i, (source, target) in enumerate((
+            (mat_hbm, mat), (table_hbm, table), (slots_hbm, slot_table),
+            (heaters_hbm, heaters), (block_hbm, block),
+        ))
+    ]
+    for load in small:
+        load.start()
     load_term = pltpu.make_async_copy(term, fields.at[0, pl.ds(slab, rows)], sem_term)
     load_term.start()
     loads = [
@@ -57,6 +67,8 @@
     lane = lax.broadcasted_iota(jnp.int32, (across, LANES), 1)
     lane_e = lax.broadcasted_iota(jnp.int32, (layers, LANES), 1)
 
+    small[0].wait()
+    small[1].wait()
     index = mat[...]
     lat = jnp.zeros(index.shape, jnp.float32)
     ver = jnp.zeros(index.shape, jnp.float32)
@@ -162,6 +174,8 @@
 
     lax.fori_loop(0, layers, coefficients, 0)
 
+    for load in small[2:]:
+        load.wait()
     cut = 4
     width = cut * LANES
     slots = slot_table[...]
@@ -276,7 +290,7 @@
                     + (gz[own, :] * z_down + mis[t, own, :])
                 )
                 if last:
-                    picked[own, :] = new
+                    adjoint[own, :] = new
                     acc = new
                     for s in range(1, steps):
                         acc = acc + fields[s, pl.ds(base + slab + b * across, across), :]
@@ -297,8 +311,6 @@
             send(t + 1)
         interior(t, last)
 
-    store = pltpu.make_async_copy(picked.at[pl.ds(0, rows)], adjoint, sem_out)
-    store.start()
     load_prof.wait()
 
     unroll = 32
@@ -306,7 +318,7 @@
     def pick(c, _):
         base = pl.multiple_of(c * unroll, unroll)
         for j in range(unroll):
-            picked[pl.ds(rows + base + j, 1), :] = total[pl.ds(block[base + j], 1), :]
+            picked[pl.ds(base + j, 1), :] = total[pl.ds(block[base + j], 1), :]
         return 0
 
     lax.fori_loop(0, entries // unroll, pick, 0)
@@ -316,7 +328,7 @@
     for c in range(entries // chunk):
         own = pl.ds(c * chunk, chunk)
         value = DT * jnp.sum(
-            picked[pl.ds(rows + c * chunk, chunk), :] * prof[own, :], axis=1, keepdims=True
+            picked[own, :] * prof[own, :], axis=1, keepdims=True
         )
         spread = one_lo[own, :] * value
         first = spread.astype(jnp.bfloat16)
@@ -357,8 +369,6 @@
         @pl.when(me > 0)
         def _():
             hop(t, False).wait_send()
-
-    store.wait()
 
     def finish(d, acc):
         deliver(d).wait_recv()
@@ -390,9 +400,8 @@
     mis = (
         misfit.reshape(steps, layers, across, nyb, LANES).swapaxes(2, 3).reshape(steps, rows, LANES)
     )
-    any_space = pl.BlockSpec(memory_space=pl.ANY)
+    hbm = pl.BlockSpec(memory_space=pltpu.HBM)
     vmem = pl.BlockSpec(memory_space=pltpu.VMEM)
-    smem = pl.BlockSpec(memory_space=pltpu.SMEM)
     f32 = jnp.float32
     adjoint, grad = pl.pallas_call(
         functools.partial(kernel, n, layers, across, nyb, steps, mats, per_owner),
@@ -400,9 +409,14 @@
             jax.ShapeDtypeStruct((rows, LANES), f32),
             jax.ShapeDtypeStruct((per_owner // LANES, LANES), f32),
         ),
-        in_specs=[any_space, any_space, vmem, smem, vmem, vmem, smem, any_space],
-        out_specs=(any_space, vmem),
+        in_specs=[hbm] * 8,
+        out_specs=(vmem, vmem),
         scratch_shapes=[
+            pltpu.VMEM((layers * across, nyb), jnp.int32),
+            pltpu.SMEM(material_table.shape, f32),
+            pltpu.VMEM((heater_slot.shape[0] // LANES, LANES), jnp.int32),
+            pltpu.VMEM((entries // LANES, LANES), jnp.int32),
+            pltpu.SMEM((entries,), jnp.int32),
             pltpu.VMEM((steps, rows + 2 * slab, LANES), f32),
             pltpu.VMEM((steps, rows, LANES), f32),
             pltpu.VMEM((entries, LANES), f32),
@@ -415,7 +429,7 @@
             pltpu.VMEM((layers * across, LANES), f32),
             pltpu.VMEM((layers * across, LANES), f32),
             pltpu.VMEM((rows, LANES), f32),
-            pltpu.VMEM((rows + entries, LANES), f32),
+            pltpu.VMEM((entries, LANES), f32),
             pltpu.VMEM((entries, LANES), f32),
             pltpu.VMEM((n * pad_rows, entries), jnp.bfloat16),
             pltpu.VMEM((n, pad_rows, LANES), f32),
@@ -427,7 +441,7 @@
             pltpu.SemaphoreType.DMA,
             pltpu.SemaphoreType.DMA((steps,)),
             pltpu.SemaphoreType.DMA,
-            pltpu.SemaphoreType.DMA,
+            pltpu.SemaphoreType.DMA((5,)),
             pltpu.SemaphoreType.DMA((steps, 2)),
             pltpu.SemaphoreType.DMA((steps, 2)),
             pltpu.SemaphoreType.DMA((n,)),

time: 50.2 us -> 49.5 us (0.986)
  Pallas kernels: 41.5 us -> 40.7 us
    pallas_call x1, Pallas kernels: 41.5 us -> 40.7 us  [on_device(): pl.pallas_call(functools.partial(kernel, n, layers, across, nyb, steps, m...]
where the time goes in v2:
time: 49.5 us; the launch traced here: 49 us
  Pallas kernels  40.7 us (82%)
  local copies, waits for them, and re-layouts  7.66 us (15%)
  between operations  0.66 us (1%)
    pallas_call x1, Pallas kernels, on_device(): pl.pallas_call(functools.partial(kernel, n, layers, across, nyb, steps, m...  40.7 us
    unnamed x16, local copies, waits for them, and re-layouts  7.66 us

profile of v2, /device:TPU:0, one launch (start us, length us, event | category | flops | bytes accessed | tf_op | source)
XLA Modules:
  0.0 49.0 jit_solution(16762885656022426080)
XLA Ops:
  0.6 0.0 copy-start
  0.6 1.2 %copy-done = f32[16,8,2048]{2,1,0:T(8,128)S(1)} copy-done((f32[16,8,2048]{2,1,0:T(8,128)S(1)}, f32[16,8,2048]{2,1,0:T(8,128)}, u32[]{:S(2)}) %copy-start) | copy-done | bytes 1048600
  1.9 0.0 copy-start.1
  1.9 1.2 %copy-done.1 = f32[2048,128]{1,0:T(8,128)S(1)} copy-done((f32[2048,128]{1,0:T(8,128)S(1)}, f32[2048,128]{1,0:T(8,128)}, u32[]{:S(2)}) %copy-start.1) | copy-done | bytes 1048600
  3.1 0.0 copy-start.2
  3.1 0.8 %copy-done.2 = s32[16,8,16]{2,1,0:T(8,128)S(1)} copy-done((s32[16,8,16]{2,1,0:T(8,128)S(1)}, s32[16,8,16]{2,1,0:T(8,128)}, u32[]{:S(2)}) %copy-start.2) | copy-done | bytes 8216
  3.9 0.0 copy-start.3
  3.9 0.8 %copy-done.3 = s32[8192]{0:T(1024)S(1)} copy-done((s32[8192]{0:T(1024)S(1)}, s32[8192]{0:T(1024)}, u32[]{:S(2)}) %copy-start.3) | copy-done | bytes 32792
  4.7 0.0 copy-start.4
  4.7 0.7 %copy-done.4 = s32[2048]{0:T(1024)S(1)} copy-done((s32[2048]{0:T(1024)S(1)}, s32[2048]{0:T(1024)}, u32[]{:S(2)}) %copy-start.4) | copy-done | bytes 8216
  5.4 0.0 copy-start.5
  5.4 0.7 %copy-done.5 = s32[2048]{0:T(1024)S(1)} copy-done((s32[2048]{0:T(1024)S(1)}, s32[2048]{0:T(1024)}, u32[]{:S(2)}) %copy-start.5) | copy-done | bytes 8216
  6.1 0.0 copy-start.6
  6.1 0.7 %copy-done.6 = f32[2,8]{1,0:T(2,128)S(1)} copy-done((f32[2,8]{1,0:T(2,128)S(1)}, f32[2,8]{1,0:T(2,128)}, u32[]{:S(2)}) %copy-start.6) | copy-done | bytes 88
  6.8 40.7 %shard_map.95 = (f32[2048,128]{1,0:T(8,128)S(1)}, f32[4,128]{1,0:T(4,128)S(1)}) custom-call(f32[2048,128]{1,0:T(8,128)S(1)} %bitcast.20, f32[4,2048,128]{2,1,0:T(8,128)} %bitcast.25, s32[128,16]{1,0:T(8,128)S(1)} %bitcast.21, f32[2,8]{1,0:T(2,128)S(1)} %copy-done.6, s32[64,128]{1,0:T(8,128)S(1)} %bitcast.22, s32[16,128]{1,0:T(8,128)S(1)} %bitcast.23, ...), custom_call_target="tpu_custom_call" | custom-call | tf_op jit(solution)/shard_map/pallas_call | solution.py:406
  47.5 1.0 %copy.12 = f32[16,8,2048]{2,1,0:T(8,128)} copy(f32[16,8,2048]{2,1,0:T(8,128)S(1)} %bitcast.19) | data formatting | bytes 2097152
  48.5 0.6 %copy.13 = f32[512]{0:T(512)} copy(f32[512]{0:T(512)S(1)} %bitcast.24) | data formatting | bytes 4096
Async XLA Ops:
  0.6 1.2 %copy-start = (f32[16,8,2048]{2,1,0:T(8,128)S(1)}, f32[16,8,2048]{2,1,0:T(8,128)}, u32[]{:S(2)}) copy-start(f32[16,8,2048]{2,1,0:T(8,128)} %param.8) | copy-start | bytes 3145732
  1.9 1.2 %copy-start.1 = (f32[2048,128]{1,0:T(8,128)S(1)}, f32[2048,128]{1,0:T(8,128)}, u32[]{:S(2)}) copy-start(f32[2048,128]{1,0:T(8,128)} %profile.1) | copy-start | bytes 3145732
  3.1 0.8 %copy-start.2 = (s32[16,8,16]{2,1,0:T(8,128)S(1)}, s32[16,8,16]{2,1,0:T(8,128)}, u32[]{:S(2)}) copy-start(s32[16,8,16]{2,1,0:T(8,128)} %param.10) | copy-start | bytes 24580
  3.9 0.8 %copy-start.3 = (s32[8192]{0:T(1024)S(1)}, s32[8192]{0:T(1024)}, u32[]{:S(2)}) copy-start(s32[8192]{0:T(1024)} %param.12) | copy-start | bytes 98308
  4.7 0.7 %copy-start.4 = (s32[2048]{0:T(1024)S(1)}, s32[2048]{0:T(1024)}, u32[]{:S(2)}) copy-start(s32[2048]{0:T(1024)} %param.13) | copy-start | bytes 24580
  5.4 0.7 %copy-start.5 = (s32[2048]{0:T(1024)S(1)}, s32[2048]{0:T(1024)}, u32[]{:S(2)}) copy-start(s32[2048]{0:T(1024)} %block_hbm.1) | copy-start | bytes 24580
  6.1 0.7 %copy-start.6 = (f32[2,8]{1,0:T(2,128)S(1)}, f32[2,8]{1,0:T(2,128)}, u32[]{:S(2)}) copy-start(f32[2,8]{1,0:T(2,128)} %table_hbm.1) | copy-start | bytes 196

commit v3 on v2

--- a/solution.py
+++ b/solution.py
@@ -21,7 +21,7 @@
     term, misfit, mat_hbm, table_hbm, slots_hbm, heaters_hbm, block_hbm, profile,
     adjoint, grad,
     mat, table, slot_table, heaters, block,
-    fields, mis, prof, gxp, gxm, gyp, gym, gz, c0, packed, vpacked, total, picked,
+    fields, mis, prof, gxp, gxm, gyp, gym, gz, c0, rim, packed, vpacked, total, picked,
     one_lo, one_hi, dense, send_lo, send_hi, from_lo, from_hi, parts,
     sem_term, sem_mis, sem_prof, sem_small, send_sems, recv_sems, out_sems, in_sems,
 ):
@@ -173,6 +173,34 @@
         return 0
 
     lax.fori_loop(0, layers, coefficients, 0)
+
+    row_e = lax.broadcasted_iota(jnp.int32, (layers, LANES), 0)
+    for s, x, inward in ((0, 0, 1), (1, across - 1, -1)):
+        lat = packed[pl.ds(x, layers, stride=across), :]
+        ver = vpacked[pl.ds(x, layers, stride=across), :]
+        g_in = half * (lat + packed[pl.ds(x + inward, layers, stride=across), :])
+        z_up = jnp.where(row_e < layers - 1, half * (ver + pltpu.roll(ver, layers - 1, 0)), 0.0)
+        z_down = jnp.where(row_e > 0, half * (ver + pltpu.roll(ver, 1, 0)), 0.0)
+        side = half * (lat + pltpu.roll(lat, LANES - 1, 1))
+        inner = DT * lat
+        center = 1.0 - z_up - z_down - g_in
+
+        def wide_e(value, b):
+            return jnp.broadcast_to(value[:, b : b + 1], (layers, LANES))
+
+        none = jnp.zeros((layers, LANES), jnp.float32)
+        sides = [none] + [wide_e(side, b) for b in range(nyb - 1)] + [none]
+        for b in range(nyb):
+            own = pl.ds(b * layers, layers)
+            y = wide_e(inner, b)
+            y_up = jnp.where(lane_e == LANES - 1, sides[b + 1], y)
+            y_down = jnp.where(lane_e == 0, sides[b], y)
+            rim[s, 0, own, :] = wide_e(center, b) - y_up - y_down
+            rim[s, 1, own, :] = y_up
+            rim[s, 2, own, :] = y_down
+            rim[s, 3, own, :] = wide_e(g_in, b)
+            rim[s, 4, own, :] = wide_e(z_up, b)
+            rim[s, 5, own, :] = wide_e(z_down, b)
 
     for load in small[2:]:
         load.wait()
@@ -216,49 +244,31 @@
     lookups = entries // width
     lax.fori_loop(0, lookups, lookup, 0)
 
-    receive(0)
-    for x, ref, arrived, outside in (
-        (0, gxm, from_lo, me == 0),
-        (across - 1, gxp, from_hi, me == n - 1),
-    ):
-        scale = jnp.where(outside, 0.0, half)
-        pair = scale * (
-            packed[pl.ds(x, layers, stride=across), :] + arrived[0, pl.ds(edge, layers), :]
-        )
-        for b in range(nyb):
-            ref[pl.ds(b * across + x, layers, stride=slab), :] = jnp.broadcast_to(
-                pair[:, b : b + 1], (layers, LANES)
-            )
-
-    def edges(t):
-        for x, inward, g_in, g_out, arrived, buffer in (
-            (0, 1, gxp, gxm, from_lo, send_lo),
-            (across - 1, -1, gxm, gxp, from_hi, send_hi),
-        ):
-            def at(ref, b, shift=0):
-                return ref[pl.ds(shift + b * across + x, layers, stride=slab), :]
-
-            def at_f(b, shift):
-                return fields[t, pl.ds(shift + b * across + x, layers, stride=slab), :]
-
-            v = [at_f(b, slab) for b in range(nyb)]
+    def edges_ready(t):
+        for s, x, inward, buffer in ((0, 0, 1, send_lo), (1, across - 1, -1, send_hi)):
+            v = [buffer[t, pl.ds(b * layers, layers), :] for b in range(nyb)]
             right = [pltpu.roll(u, LANES - 1, 1) for u in v]
             left = [pltpu.roll(u, 1, 1) for u in v]
             for b in range(nyb):
+                own = pl.ds(b * layers, layers)
                 y_up = jnp.where(lane_e == LANES - 1, right[min(b + 1, nyb - 1)], right[b])
                 y_down = jnp.where(lane_e == 0, left[max(b - 1, 0)], left[b])
-                here = v[b]
-                inner = at_f(b, slab + inward)
-                outer = arrived[t, pl.ds(b * layers, layers), :]
-                new = (
-                    (at(c0, b) * here + at(gyp, b) * y_up)
-                    + (at(gym, b) * y_down + at(g_in, b) * (inner - here))
+                inner = fields[t, pl.ds(slab + b * across + x + inward, layers, stride=slab), :]
+                buffer[t + 1, own, :] = (
+                    (rim[s, 0, own, :] * v[b] + rim[s, 1, own, :] * y_up)
+                    + (rim[s, 2, own, :] * y_down + rim[s, 3, own, :] * inner)
                 ) + (
-                    (at(g_out, b) * (outer - here) + at(gz, b, slab) * at_f(b, 2 * slab))
-                    + (at(gz, b) * at_f(b, 0)
-                       + mis[t, pl.ds(b * across + x, layers, stride=slab), :])
+                    (rim[s, 4, own, :] * pltpu.roll(v[b], layers - 1, 0)
+                     + rim[s, 5, own, :] * pltpu.roll(v[b], 1, 0))
+                    + mis[t, pl.ds(b * across + x, layers, stride=slab), :]
                 )
-                buffer[t + 1, pl.ds(b * layers, layers), :] = new
+
+    def edges_done(t):
+        whole = pl.ds(0, edge)
+        for s, arrived, buffer in ((0, from_lo, send_lo), (1, from_hi, send_hi)):
+            buffer[t + 1, whole, :] = buffer[t + 1, whole, :] + rim[s, 6, :, :] * (
+                arrived[t, whole, :] - buffer[t, whole, :]
+            )
 
     def interior(t, last):
         def body(k, _):
@@ -301,13 +311,31 @@
 
         lax.fori_loop(0, layers, body, 0)
 
+    loads[0].wait()
+    edges_ready(0)
+    receive(0)
+    for s, x, ref, arrived, outside in (
+        (0, 0, gxm, from_lo, me == 0),
+        (1, across - 1, gxp, from_hi, me == n - 1),
+    ):
+        scale = jnp.where(outside, 0.0, half)
+        pair = scale * (
+            packed[pl.ds(x, layers, stride=across), :] + arrived[0, pl.ds(edge, layers), :]
+        )
+        for b in range(nyb):
+            value = jnp.broadcast_to(pair[:, b : b + 1], (layers, LANES))
+            ref[pl.ds(b * across + x, layers, stride=slab), :] = value
+            rim[s, 6, pl.ds(b * layers, layers), :] = value
+
     for t in range(steps):
         last = t == steps - 1
-        loads[t].wait()
         if t > 0:
+            loads[t].wait()
+            if not last:
+                edges_ready(t)
             receive(t)
         if not last:
-            edges(t)
+            edges_done(t)
             send(t + 1)
         interior(t, last)
 
@@ -426,6 +454,7 @@
             pltpu.VMEM((rows, LANES), f32),
             pltpu.VMEM((rows + slab, LANES), f32),
             pltpu.VMEM((rows, LANES), f32),
+            pltpu.VMEM((2, 7, edge, LANES), f32),
             pltpu.VMEM((layers * across, LANES), f32),
             pltpu.VMEM((layers * across, LANES), f32),
             pltpu.VMEM((rows, LANES), f32),
@@ -448,7 +477,7 @@
             pltpu.SemaphoreType.DMA((n,)),
         ],
         compiler_params=pltpu.CompilerParams(
-            collective_id=0, has_side_effects=True, vmem_limit_bytes=48 * 1024 * 1024
+            collective_id=0, has_side_effects=True, vmem_limit_bytes=64 * 1024 * 1024
         ),
     )(
         term,

time: 49.5 us -> 39.6 us (0.80)
  Pallas kernels: 40.7 us -> 35.3 us
  local copies, waits for them, and re-layouts: 7.66 us -> 3.55 us
    pallas_call x1, Pallas kernels: 40.7 us -> 35.3 us  [on_device(): pl.pallas_call(functools.partial(kernel, n, layers, across, nyb, steps, m...]
    unnamed x16 -> x2, local copies, waits for them, and re-layouts: 7.66 us -> 3.55 us
where the time goes in v3:
time: 39.6 us; the launch traced here: 39.4 us
  Pallas kernels  35.3 us (89%)
  local copies, waits for them, and re-layouts  3.55 us (9%)
  between operations  0.64 us (2%)
    pallas_call x1, Pallas kernels, on_device(): pl.pallas_call(functools.partial(kernel, n, layers, across, nyb, steps, m...  35.3 us
    unnamed x2, local copies, waits for them, and re-layouts  3.55 us

profile of v3, /device:TPU:0, one launch (start us, length us, event | category | flops | bytes accessed | tf_op | source)
XLA Modules:
  0.0 39.4 jit_solution(14154801577365979863)
XLA Ops:
  0.6 35.3 %shard_map.95 = (f32[2048,128]{1,0:T(8,128)}, f32[4,128]{1,0:T(4,128)}) custom-call(f32[2048,128]{1,0:T(8,128)} %bitcast.21, f32[4,2048,128]{2,1,0:T(8,128)} %bitcast.19, s32[128,16]{1,0:T(8,128)} %bitcast.22, f32[2,8]{1,0:T(2,128)} %table_hbm.1, s32[64,128]{1,0:T(8,128)} %bitcast.23, s32[16,128]{1,0:T(8,128)} %bitcast.24, s32[2048]{0:T(1024)} %block_hbm.1, ...), custom_call_target="tpu_custom_call" | custom-call | tf_op jit(solution)/shard_map/pallas_call | solution.py:434
  35.9 2.3 %copy.12 = f32[16,8,2048]{2,1,0:T(8,128)} copy(f32[16,8,2048]{2,1,0:T(8,128)} %bitcast.20) | data formatting | bytes 2097152
  38.2 1.3 %copy.13 = f32[512]{0:T(512)} copy(f32[512]{0:T(512)} %bitcast.25) | data formatting | bytes 4096

commit v4 on v3

--- a/solution.py
+++ b/solution.py
@@ -21,9 +21,9 @@
     term, misfit, mat_hbm, table_hbm, slots_hbm, heaters_hbm, block_hbm, profile,
     adjoint, grad,
     mat, table, slot_table, heaters, block,
-    fields, mis, prof, gxp, gxm, gyp, gym, gz, c0, rim, packed, vpacked, total, picked,
+    fields, mis, prof, gxp, gxm, gyp, gym, gz, c0, rim, packed, vpacked, total, picked, final,
     one_lo, one_hi, dense, send_lo, send_hi, from_lo, from_hi, parts,
-    sem_term, sem_mis, sem_prof, sem_small, send_sems, recv_sems, out_sems, in_sems,
+    sem_term, sem_mis, sem_prof, sem_small, send_sems, recv_sems, out_sems, in_sems, sem_out,
 ):
     me = lax.axis_index("gx")
     slab = nyb * across
@@ -42,7 +42,7 @@
         )
         return 0
 
-    lax.fori_loop(1, n, greet, 0)
+    lax.fori_loop(1, n, greet, 0, unroll=n <= 16)
 
     small = [
         pltpu.make_async_copy(source, target, sem_small.at[i])
@@ -132,6 +132,7 @@
                 0, pl.ds(slab + b * across + x, layers, stride=slab), :
             ]
         buffer[0, pl.ds(edge, layers), :] = packed[pl.ds(x, layers, stride=across), :]
+
     pl.semaphore_wait(barrier, n - 1)
     send(0)
 
@@ -242,7 +243,8 @@
         return 0
 
     lookups = entries // width
-    lax.fori_loop(0, lookups, lookup, 0)
+    early = lookups - (steps - 1)
+    lax.fori_loop(0, early, lookup, 0)
 
     def edges_ready(t):
         for s, x, inward, buffer in ((0, 0, 1, send_lo), (1, across - 1, -1, send_hi)):
@@ -273,14 +275,17 @@
     def interior(t, last):
         def body(k, _):
             base = pl.multiple_of(k * slab, slab)
-            v = [fields[t, pl.ds(base + slab + b * across, across), :] for b in range(nyb)]
-            right = [pltpu.roll(u, LANES - 1, 1) for u in v]
-            left = [pltpu.roll(u, 1, 1) for u in v]
+            def load(b):
+                u = fields[t, pl.ds(base + slab + b * across, across), :]
+                return u, pltpu.roll(u, LANES - 1, 1), pltpu.roll(u, 1, 1)
+
+            here, right, left = load(0)
+            left_before = left
             for b in range(nyb):
                 own = pl.ds(base + b * across, across)
-                here = v[b]
-                y_up = jnp.where(lane == LANES - 1, right[min(b + 1, nyb - 1)], right[b])
-                y_down = jnp.where(lane == 0, left[max(b - 1, 0)], left[b])
+                following = load(b + 1) if b + 1 < nyb else (here, right, left)
+                y_up = jnp.where(lane == LANES - 1, following[1], right)
+                y_down = jnp.where(lane == 0, left_before, left)
                 x_up = jnp.where(
                     sub == across - 1,
                     from_hi[t, pl.ds(b * layers + k, 1), :],
@@ -300,13 +305,15 @@
                     + (gz[own, :] * z_down + mis[t, own, :])
                 )
                 if last:
-                    adjoint[own, :] = new
+                    final[own, :] = new
                     acc = new
                     for s in range(1, steps):
                         acc = acc + fields[s, pl.ds(base + slab + b * across, across), :]
                     total[pl.ds(base + b, across, stride=nyb), :] = acc
                 else:
                     fields[t + 1, pl.ds(base + slab + b * across, across), :] = new
+                left_before = left
+                here, right, left = following
             return 0
 
         lax.fori_loop(0, layers, body, 0)
@@ -338,7 +345,11 @@
             edges_done(t)
             send(t + 1)
         interior(t, last)
-
+        if not last:
+            lookup(early + t, 0)
+
+    store = pltpu.make_async_copy(final, adjoint, sem_out)
+    store.start()
     load_prof.wait()
 
     unroll = 32
@@ -387,7 +398,7 @@
         deliver(d).start()
         return 0
 
-    lax.fori_loop(1, n, start, 0)
+    lax.fori_loop(1, n, start, 0, unroll=n <= 16)
 
     for t in range(steps):
         @pl.when(me < n - 1)
@@ -402,14 +413,35 @@
         deliver(d).wait_recv()
         return acc + parts[d]
 
-    result = lax.fori_loop(1, n, finish, dense[me])
+    store.wait()
+    result = lax.fori_loop(1, n, finish, dense[me], unroll=n <= 16)
     grad[...] = result[:owner_rows]
 
     def drain(d, _):
         deliver(d).wait_send()
         return 0
 
-    lax.fori_loop(1, n, drain, 0)
+    lax.fori_loop(1, n, drain, 0, unroll=n <= 16)
+
+
+PARTS = 4
+
+
+def hand_on(adjoint_in, grad_in, adjoint, grad, held, held_grad, sems):
+    size = adjoint.shape[0] // PARTS
+    moves = [(grad_in, held_grad, grad)]
+    for p in range(PARTS):
+        part = pl.ds(p * size, size)
+        moves.append((adjoint_in.at[part], held.at[part], adjoint.at[part]))
+    loads = [pltpu.make_async_copy(a, b, sems.at[i, 0]) for i, (a, b, _) in enumerate(moves)]
+    stores = [pltpu.make_async_copy(b, c, sems.at[i, 1]) for i, (_, b, c) in enumerate(moves)]
+    for load in loads:
+        load.start()
+    for load, store in zip(loads, stores):
+        load.wait()
+        store.start()
+    for store in stores:
+        store.wait()
 
 
 def on_device(
@@ -438,7 +470,7 @@
             jax.ShapeDtypeStruct((per_owner // LANES, LANES), f32),
         ),
         in_specs=[hbm] * 8,
-        out_specs=(vmem, vmem),
+        out_specs=(hbm, vmem),
         scratch_shapes=[
             pltpu.VMEM((layers * across, nyb), jnp.int32),
             pltpu.SMEM(material_table.shape, f32),
@@ -459,6 +491,7 @@
             pltpu.VMEM((layers * across, LANES), f32),
             pltpu.VMEM((rows, LANES), f32),
             pltpu.VMEM((entries, LANES), f32),
+            pltpu.VMEM((rows, LANES), f32),
             pltpu.VMEM((entries, LANES), f32),
             pltpu.VMEM((n * pad_rows, entries), jnp.bfloat16),
             pltpu.VMEM((n, pad_rows, LANES), f32),
@@ -475,6 +508,7 @@
             pltpu.SemaphoreType.DMA((steps, 2)),
             pltpu.SemaphoreType.DMA((n,)),
             pltpu.SemaphoreType.DMA((n,)),
+            pltpu.SemaphoreType.DMA,
         ],
         compiler_params=pltpu.CompilerParams(
             collective_id=0, has_side_effects=True, vmem_limit_bytes=64 * 1024 * 1024
@@ -489,6 +523,21 @@
         entry_block,
         profile,
     )
+    adjoint, grad = pl.pallas_call(
+        hand_on,
+        out_shape=(
+            jax.ShapeDtypeStruct(adjoint.shape, f32),
+            jax.ShapeDtypeStruct(grad.shape, f32),
+        ),
+        in_specs=[hbm] * 2,
+        out_specs=(hbm, hbm),
+        scratch_shapes=[
+            pltpu.VMEM(adjoint.shape, f32),
+            pltpu.VMEM(grad.shape, f32),
+            pltpu.SemaphoreType.DMA((PARTS + 1, 2)),
+        ],
+        compiler_params=pltpu.CompilerParams(vmem_limit_bytes=60 * 1024 * 1024),
+    )(adjoint, grad)
     adjoint = adjoint.reshape(layers, nyb, across, LANES).swapaxes(1, 2).reshape(terminal.shape)
     return (adjoint, grad.reshape(per_owner))
 

time: 39.6 us -> 36.1 us (0.912)
  local copies, waits for them, and re-layouts: 3.55 us -> 0 us
    unnamed x2 -> x0, local copies, waits for them, and re-layouts: 3.55 us -> none
    pallas_call x0 -> x1, Pallas kernels: none -> 2 us  [on_device(): pl.pallas_call(hand_on, out_shape=(jax.ShapeDtypeStruct(adjoint.shape, f3...]
    pallas_call x1, Pallas kernels: 35.3 us -> 33.3 us  [on_device(): pl.pallas_call(functools.partial(kernel, n, layers, across, nyb, steps, m...]
where the time goes in v4:
time: 36.1 us; the launch traced here: 35.9 us
  Pallas kernels  35.3 us (98%)
  between operations  0.64 us (2%)
    pallas_call x1, Pallas kernels, on_device(): pl.pallas_call(functools.partial(kernel, n, layers, across, nyb, steps, m...  33.3 us
    pallas_call x1, Pallas kernels, on_device(): pl.pallas_call(hand_on, out_shape=(jax.ShapeDtypeStruct(adjoint.shape, f3...  2 us

profile of v4, /device:TPU:0, one launch (start us, length us, event | category | flops | bytes accessed | tf_op | source)
XLA Modules:
  0.0 35.9 jit_solution(8518836671823246764)
XLA Ops:
  0.6 33.3 %shard_map.95 = (f32[2048,128]{1,0:T(8,128)}, f32[4,128]{1,0:T(4,128)}) custom-call(f32[2048,128]{1,0:T(8,128)} %bitcast.20, f32[4,2048,128]{2,1,0:T(8,128)} %bitcast.19, s32[128,16]{1,0:T(8,128)} %bitcast.21, f32[2,8]{1,0:T(2,128)} %table_hbm.1, s32[64,128]{1,0:T(8,128)} %bitcast.22, s32[16,128]{1,0:T(8,128)} %bitcast.23, s32[2048]{0:T(1024)} %block_hbm.1, ...), custom_call_target="tpu_custom_call" | custom-call | tf_op jit(solution)/shard_map/pallas_call | solution.py:466
  33.9 2.0 %shard_map.96 = (f32[2048,128]{1,0:T(8,128)}, f32[4,128]{1,0:T(4,128)}) custom-call(f32[2048,128]{1,0:T(8,128)} %get-tuple-element.6.adjoint_in, f32[4,128]{1,0:T(4,128)} %get-tuple-element.7.grad_in), custom_call_target="tpu_custom_call" | custom-call | tf_op jit(solution)/shard_map/pallas_call | solution.py:526
